TPU v7x, 256 devices: a whole 4x4x8 slice. The times are simulated.
256 devices in a mesh: tm: 16 (over y_lo, z), gx: 4 (over y_hi, core), gy: 4 (over x).
Axes of the slice: x: 4, y: 4 (y_hi: 2, y_lo: 2; y = y_hi * 2 + y_lo), z: 8, core: 2. Of those that a mesh axis runs over, the one named last changes fastest.
Arguments:
- initial_temp: float32 [64, 32, 512], P(None, 'gx', 'gy'), may hold values from -4 to 4
- conductivity: float32 [64, 32, 512], P(None, 'gx', 'gy'), may hold values from 0.5 to 2
- vert_cond: float32 [64], replicated, may hold values from 0.5 to 2
- borehole_cells: int32 [4, 4, 16], P('gx', 'gy'), may hold values from 0 to 1023
- borehole_profiles: int32 [4, 4, 16], P('gx', 'gy'), may hold values from 0 to 7
- heat_table: float32 [8, 16], P(None, 'tm'), may hold values from 0.1 to 0.8
Outputs:
- end_temp: float32 [16, 64, 32, 512], P('tm', None, 'gx', 'gy')
Inputs may be any that keep to these rules, and one draw needn't show every extreme that they name: `borehole_cells`: cell x * 128 + y of the lateral tile of its (gx, gy) block; cells may repeat, and then their heat adds.
All inputs are finite; a program needn't handle non-finite values.
Results may differ from a plain program's by a relative error of at most 0.0003.
Values sent between devices are 32-bit elements; how exact they have to be, the bound alone decides.
No kernel may reach another device: no remote copies, remote signals or barrier semaphores. Data moves between devices by JAX's collectives and lax.ppermute only.
A program may use at most 128 MiB of HBM per device.

v0:
```python
import math

import jax
import jax.numpy as jnp
from jax import lax
from jax.sharding import PartitionSpec as P

ITERS = 2


LATERAL = 0.3
VERTICAL = 4.0
SPAN = 1.0
FINE_NODES = [0.0, (1.0 - math.sqrt(3.0 / 7.0)) / 2.0, 0.5, (1.0 + math.sqrt(3.0 / 7.0)) / 2.0, 1.0]
COARSE_NODES = [0.0, 0.5, 1.0]


def padded(x, sides, width):
    for axis, dim in sides:
        size, length = (lax.axis_size(axis), x.shape[dim])
        up = [(i, (i + 1) % size) for i in range(size - 1)]
        down = [(j, i) for i, j in up]
        last = lax.slice_in_dim(x, length - width, length, axis=dim)
        first = lax.slice_in_dim(x, 0, width, axis=dim)
        before = lax.ppermute(last, axis, up)
        after = lax.ppermute(first, axis, down)
        x = jnp.concatenate([before, x, after], axis=dim)
    return x


def from_behind(value, axis, steps):
    count = lax.axis_size(axis)
    first, last = (max(0, -steps), min(count, count - steps))
    return lax.ppermute(value, axis, [(source, source + steps) for source in range(first, last)])


def basis_coeffs(times_list, basis_index):
    coeffs = [1.0]
    denominator = 1.0
    for other_index in range(len(times_list)):
        if other_index != basis_index:
            other_time = times_list[other_index]
            widened = [0.0] * (len(coeffs) + 1)
            for power in range(len(coeffs)):
                widened[power + 1] = widened[power + 1] + coeffs[power]
                widened[power] = widened[power] - other_time * coeffs[power]
            coeffs = widened
            denominator = denominator * (times_list[basis_index] - other_time)
    return [entry / denominator for entry in coeffs]


def poly_value(coeffs, point):
    total = 0.0
    for power in range(len(coeffs)):
        total = total + coeffs[power] * point**power
    return total


def poly_integral(coeffs, lower, upper):
    total = 0.0
    for power in range(len(coeffs)):
        total = total + coeffs[power] * (upper ** (power + 1) - lower ** (power + 1)) / (power + 1)
    return total


def node_integrals(times_list):
    integrals = []
    for interval in range(len(times_list) - 1):
        entries = []
        for basis_index in range(len(times_list)):
            entries.append(
                float(
                    poly_integral(
                        basis_coeffs(times_list, basis_index),
                        times_list[interval],
                        times_list[interval + 1],
                    )
                )
            )
        integrals.append(entries)
    return integrals


def node_values(times_list, targets):
    return [
        [
            float(poly_value(basis_coeffs(times_list, basis_index), target))
            for basis_index in range(len(times_list))
        ]
        for target in targets
    ]


def vertical_matrix(vert_cond):
    depth = vert_cond.shape[0]
    lower_faces = jnp.concatenate([vert_cond[1:], jnp.zeros((1,), jnp.float32)])
    centre = -VERTICAL * (vert_cond + lower_faces)
    levels = jnp.arange(depth, dtype=jnp.int32)
    row_index = levels[:, None]
    col_index = levels[None, :]
    matrix = jnp.where(row_index == col_index, centre[:, None], 0.0)
    matrix = matrix + jnp.where(col_index == row_index - 1, VERTICAL * vert_cond[:, None], 0.0)
    matrix = matrix + jnp.where(col_index == row_index + 1, VERTICAL * lower_faces[:, None], 0.0)
    return matrix


def propagator(matrix, interval):
    depth = matrix.shape[0]
    identity = jnp.eye(depth, dtype=matrix.dtype)
    factor = jnp.linalg.cholesky(identity - interval * matrix)
    halfway = jax.scipy.linalg.solve_triangular(factor, identity, lower=True)
    return jax.scipy.linalg.solve_triangular(factor, halfway, trans=1, lower=True)


def column_apply(matrix, volume):
    depth = volume.shape[0]
    flattened = volume.reshape(depth, -1)
    product = jnp.dot(
        matrix, flattened, precision=lax.Precision.HIGHEST, preferred_element_type=jnp.float32
    )
    return product.reshape(volume.shape)


def lateral_term(extended, conduct, coefficient):
    centre = extended[:, 1:-1, 1:-1]
    beside_all = (
        extended[:, 2:, 1:-1]
        + extended[:, :-2, 1:-1]
        + extended[:, 1:-1, 2:]
        + extended[:, 1:-1, :-2]
    )
    return coefficient * conduct * (beside_all - 4.0 * centre)


def interior(volume, margin):
    return volume[:, margin : volume.shape[1] - margin, margin : volume.shape[2] - margin]


def restrict(volume):
    depth, rows_x, rows_y = volume.shape
    return jnp.mean(volume.reshape(depth, rows_x // 2, 2, rows_y // 2, 2), axis=(2, 4))


def restrict_plane(heat_plane):
    rows_x, rows_y = heat_plane.shape
    return jnp.mean(heat_plane.reshape(rows_x // 2, 2, rows_y // 2, 2), axis=(1, 3))


def expand(volume):
    return jnp.repeat(jnp.repeat(volume, 2, axis=1), 2, axis=2)


def integrate(integrals, totals):
    interval_sums = []
    for interval in range(len(integrals)):
        running = integrals[interval][0] * totals[0]
        for basis_index in range(1, len(totals)):
            running = running + integrals[interval][basis_index] * totals[basis_index]
        interval_sums.append(running)
    return interval_sums


def node_sweep(
    start_value, start_explicit, start_implicit, known_terms, propagators, step_lengths, explicit_fn
):
    states = [start_value]
    explicit_list = [start_explicit]
    implicit_list = [start_implicit]
    for interval in range(len(step_lengths)):
        rhs_value = (
            states[interval]
            + step_lengths[interval] * explicit_list[interval]
            + known_terms[interval]
        )
        advanced = column_apply(propagators[interval], rhs_value)
        implicit_list.append((advanced - rhs_value) / step_lengths[interval])
        states.append(advanced)
        explicit_list.append(explicit_fn(advanced))
    return (states, explicit_list, implicit_list)


def blend(weights, fine_index, deltas):
    return (
        weights[fine_index][0] * deltas[0]
        + weights[fine_index][1] * deltas[1]
        + weights[fine_index][2] * deltas[2]
    )


def correct(values_list, deltas, weights):
    return [
        values_list[fine_index] + expand(blend(weights, fine_index, deltas))
        for fine_index in range(len(values_list))
    ]


def on_device(initial_temp, conductivity, vert_cond, borehole_cells, borehole_profiles, heat_table):
    matrix = vertical_matrix(vert_cond)
    fine_steps = [SPAN * (FINE_NODES[interval + 1] - FINE_NODES[interval]) for interval in range(4)]
    coarse_steps = [
        SPAN * (COARSE_NODES[interval + 1] - COARSE_NODES[interval]) for interval in range(2)
    ]
    fine_props = [propagator(matrix, step_length) for step_length in fine_steps]
    coarse_props = [propagator(matrix, step_length) for step_length in coarse_steps]
    fine_integrals = node_integrals(FINE_NODES)
    weights = node_values(COARSE_NODES, FINE_NODES)
    depth, rows_x, rows_y = initial_temp.shape
    is_first = lax.axis_index("tm") == 0
    bore_cells = borehole_cells.reshape(-1)
    profiles = borehole_profiles.reshape(-1)
    rates_here = heat_table[:, 0]
    profile_match = profiles[:, None] == jnp.arange(heat_table.shape[0], dtype=jnp.int32)[None, :]
    borehole_rate = jnp.sum(jnp.where(profile_match, rates_here[None, :], 0.0), axis=1)
    cell_match = bore_cells[:, None] == jnp.arange(rows_x * rows_y, dtype=jnp.int32)[None, :]
    heat_plane = jnp.sum(jnp.where(cell_match, borehole_rate[:, None], 0.0), axis=0).reshape(
        rows_x, rows_y
    )
    coarse_plane = restrict_plane(heat_plane)
    coarse_conduct = restrict(conductivity)
    conduct_wide = padded(coarse_conduct, (("gx", 1), ("gy", 2)), 2)

    def explicit_fine(volume):
        extended = padded(volume, (("gx", 1), ("gy", 2)), 1)
        return lateral_term(extended, conductivity, LATERAL)

    explicit_init = explicit_fine(initial_temp)
    implicit_init = column_apply(matrix, initial_temp)
    fine_state = [initial_temp] * 5
    fine_explicit = [explicit_init] * 5
    fine_implicit = [implicit_init] * 5
    start_value = initial_temp
    start_explicit = explicit_init
    start_implicit = implicit_init
    for iteration in range(ITERS):
        if iteration > 0:
            start_explicit = explicit_fine(start_value)
            start_implicit = column_apply(matrix, start_value)
        old_sums = integrate(
            fine_integrals,
            [fine_explicit[node_index] + fine_implicit[node_index] for node_index in range(5)],
        )
        known_terms = [
            SPAN * old_sums[interval]
            + fine_steps[interval] * heat_plane
            - fine_steps[interval] * (fine_explicit[interval] + fine_implicit[interval + 1])
            for interval in range(4)
        ]
        fine_state, fine_explicit, fine_implicit = node_sweep(
            start_value,
            start_explicit,
            start_implicit,
            known_terms,
            fine_props,
            fine_steps,
            explicit_fine,
        )
        new_sums = integrate(
            fine_integrals,
            [fine_explicit[node_index] + fine_implicit[node_index] for node_index in range(5)],
        )
        coarse_old = [restrict(fine_state[0]), restrict(fine_state[2]), restrict(fine_state[4])]
        coarse_sources = [
            SPAN * restrict(new_sums[2 * interval] + new_sums[2 * interval + 1])
            + coarse_steps[interval] * coarse_plane
            for interval in range(2)
        ]
        coarse_implicit_old = [column_apply(matrix, member) for member in coarse_old]
        stacked = padded(jnp.stack(coarse_old), (("gx", 2), ("gy", 3)), 1)
        coarse_explicit_old = [
            lateral_term(stacked[member], coarse_conduct, LATERAL / 4.0) for member in range(3)
        ]
        known_here = [
            coarse_sources[interval]
            - coarse_steps[interval]
            * (coarse_explicit_old[interval] + coarse_implicit_old[interval + 1])
            for interval in range(2)
        ]
        known_wide = padded(jnp.stack(known_here), (("gx", 2), ("gy", 3)), 2)

        def widen_start(chain_start):
            return padded(chain_start, (("gx", 1), ("gy", 2)), 3)

        def coarse_sweep(widened):
            chain_start = interior(widened, 3)
            explicit_zero = lateral_term(widened, conduct_wide, LATERAL / 4.0)
            rhs_zero = interior(widened, 1) + coarse_steps[0] * explicit_zero + known_wide[0]
            node_one = column_apply(coarse_props[0], rhs_zero)
            implicit_one = (node_one - rhs_zero) / coarse_steps[0]
            explicit_one = lateral_term(node_one, interior(conduct_wide, 1), LATERAL / 4.0)
            rhs_one = (
                interior(node_one, 1) + coarse_steps[1] * explicit_one + interior(known_wide[1], 1)
            )
            node_two = column_apply(coarse_props[1], rhs_one)
            implicit_two = (node_two - rhs_one) / coarse_steps[1]
            explicit_two = lateral_term(node_two, interior(conduct_wide, 2), LATERAL / 4.0)
            return (
                chain_start,
                interior(node_one, 2),
                interior(node_two, 1),
                interior(explicit_zero, 2),
                interior(explicit_one, 1),
                explicit_two,
                column_apply(matrix, chain_start),
                interior(implicit_one, 2),
                interior(implicit_two, 1),
            )

        first_widened = widen_start(coarse_old[0])
        first_section = coarse_sweep(first_widened)

        def chain_section(counter, carried):
            received = from_behind(carried[2], "tm", 1)
            return coarse_sweep(widen_start(jnp.where(is_first, coarse_old[0], received)))

        final_section = lax.fori_loop(0, lax.axis_size("tm") - 1, chain_section, first_section)
        delta_state = [final_section[member] - coarse_old[member] for member in range(3)]
        delta_explicit = [
            final_section[3 + member] - coarse_explicit_old[member] for member in range(3)
        ]
        delta_implicit = [
            final_section[6 + member] - coarse_implicit_old[member] for member in range(3)
        ]
        fine_state = correct(fine_state, delta_state, weights)
        fine_explicit = correct(fine_explicit, delta_explicit, weights)
        fine_implicit = correct(fine_implicit, delta_implicit, weights)
        if iteration + 1 < ITERS:
            handed = from_behind(fine_state[4], "tm", 1)
            start_value = jnp.where(is_first, initial_temp, handed)
    return fine_state[4][None]


def solution(mesh):
    placed = (
        P(None, "gx", "gy"),
        P(None, "gx", "gy"),
        P(),
        P("gx", "gy", None),
        P("gx", "gy", None),
        P(None, "tm"),
    )
    return jax.shard_map(
        on_device, mesh=mesh, in_specs=placed, out_specs=P("tm", None, "gx", "gy"), check_vma=False
    )
```

profile of v0, /device:TPU:30, one launch (start us, length us, event | category | flops | bytes accessed | tf_op | source)
XLA Modules:
  0.0 1596.0 jit_solution(15433424770690858303)
XLA Ops:
  108.0 6.0 collective-permute-start.20
  233.5 599.1 %while.44 = (s32[]{:T(128)}, f32[64,4,64]{2,1,0:T(4,128)}, f32[64,4,64]{2,1,0:T(4,128)}, f32[64,4,64]{2,1,0:T(4,128)S(1)}, f32[64,4,64]{2,1,0:T(4,128)}, /*index...) while((s32[]{:T(128)}, f32[64,4,64]{2,1,0:T(4,128)}, ...), condition=%wide.region_12.16_spmd.clone, body=%wide.region_11.15_spmd.clone.sunk | while | flops 59877888 | bytes 8436478 | solution.py:315
  237.3 7.1 collective-permute-done.5
  279.5 7.0 collective-permute-done.5
  319.0 7.0 collective-permute-done.5
  358.7 7.0 collective-permute-done.5
  398.3 7.0 collective-permute-done.5
  438.0 7.0 collective-permute-done.5
  477.6 7.0 collective-permute-done.5
  517.3 7.0 collective-permute-done.5
  556.9 7.0 collective-permute-done.5
  596.6 7.0 collective-permute-done.5
  636.2 7.0 collective-permute-done.5
  675.9 7.0 collective-permute-done.5
  715.5 7.0 collective-permute-done.5
  755.2 7.0 collective-permute-done.5
  794.9 7.0 collective-permute-done.5
  958.0 6.2 collective-permute-start.67
  1025.6 565.6 %while.43 = (s32[]{:T(128)}, f32[64,4,64]{2,1,0:T(4,128)}, f32[64,4,64]{2,1,0:T(4,128)}, f32[64,4,64]{2,1,0:T(4,128)S(1)}, pred[]{:T(512)}, /*index=5*/f32[64,4,...) while((s32[]{:T(128)}, f32[64,4,64]{2,1,0:T(4,128)}, ...), condition=%wide.region_19.23_spmd, body=%wide.region_18.22_spmd.sunk | while | flops 47081984 | bytes 6556034 | solution.py:315
  1027.5 7.0 collective-permute-done
  1065.7 7.0 collective-permute-done
  1087.7 6.2 collective-permute-done.3
  1103.9 7.0 collective-permute-done
  1125.3 6.2 collective-permute-done.3
  1141.5 7.0 collective-permute-done
  1163.0 6.2 collective-permute-done.3
  1179.1 7.0 collective-permute-done
  1200.6 6.2 collective-permute-done.3
  1216.7 7.0 collective-permute-done
  1238.2 6.2 collective-permute-done.3
  1254.4 7.0 collective-permute-done
  1275.9 6.2 collective-permute-done.3
  1292.0 7.0 collective-permute-done
  1313.5 6.2 collective-permute-done.3
  1329.7 7.0 collective-permute-done
  1351.1 6.2 collective-permute-done.3
  1367.3 7.0 collective-permute-done
  1388.8 6.2 collective-permute-done.3
  1404.9 7.0 collective-permute-done
  1426.4 6.2 collective-permute-done.3
  1442.6 7.0 collective-permute-done
  1464.0 6.2 collective-permute-done.3
  1480.2 7.0 collective-permute-done
  1501.7 6.2 collective-permute-done.3
  1517.8 7.0 collective-permute-done
  1539.3 6.2 collective-permute-done.3
  1555.5 7.0 collective-permute-done
  1576.9 6.2 collective-permute-done.3
  (1751 shorter events, 1276.8 us)
Async XLA Ops:
  1.1 53.4 %collective-permute-start.11 = (f32[64,1,128]{2,0,1:T(8,128)S(1)}, f32[64,1,128]{2,0,1:T(8,128)S(1)}, u32[]{:S(2)}, u32[]{:S(2)}) collective-permute-start(f32[64,1,128]{2,0,1:T(8,128)S(1)} %get-tuple-element.578), channel_id=1, source_target_pairs={{0,4},{4,8},{8,12},{1,5},{5,9},{9,13},{2,6},{6,10},{10,14},{3,7},{... | collective-permute-start | bytes 98312 | tf_op jit(solution)/shard_map/ppermute | solution.py:25
  3.0 51.6 %collective-permute-start.10 = (f32[64,1,128]{2,0,1:T(8,128)S(1)}, f32[64,1,128]{2,0,1:T(8,128)S(1)}, u32[]{:S(2)}, u32[]{:S(2)}) collective-permute-start(f32[64,1,128]{2,0,1:T(8,128)S(1)} %get-tuple-element.577), channel_id=1, source_target_pairs={{4,0},{8,4},{12,8},{5,1},{9,5},{13,9},{6,2},{10,6},{14,10},{7,3},{... | collective-permute-start | bytes 98312 | tf_op jit(solution)/shard_map/ppermute | solution.py:26
  10.2 83.5 %collective-permute-start.27 = (f32[64,3,64]{0,2,1:T(8,128)}, f32[64,3,64]{0,2,1:T(8,128)S(1)}, u32[]{:S(2)}, u32[]{:S(2)}) collective-permute-start(f32[64,3,64]{0,2,1:T(8,128)} %get-tuple-element.592), channel_id=1, source_target_pairs={{4,0},{8,4},{12,8},{5,1},{9,5},{13,9},{6,2},{10,6},{14,10},{7,3},{... | collective-permute-start | bytes 147464 | tf_op jit(solution)/shard_map/ppermute | solution.py:26
  12.2 81.6 %collective-permute-start.26 = (f32[64,3,64]{0,2,1:T(8,128)S(1)}, f32[64,3,64]{0,2,1:T(8,128)S(1)}, u32[]{:S(2)}, u32[]{:S(2)}) collective-permute-start(f32[64,3,64]{0,2,1:T(8,128)S(1)} %get-tuple-element.591), channel_id=1, source_target_pairs={{0,4},{4,8},{8,12},{1,5},{5,9},{9,13},{2,6},{6,10},{10,14},{3,7},{... | collective-permute-start | bytes 147464 | tf_op jit(solution)/shard_map/ppermute | solution.py:25
  91.8 12.4 collective-permute-start.19
  93.7 20.3 %collective-permute-start.29 = (f32[64,10,3]{0,2,1:T(4,128)S(1)}, f32[64,10,3]{0,2,1:T(4,128)S(1)}, u32[]{:S(2)}, u32[]{:S(2)}) collective-permute-start(f32[64,10,3]{0,2,1:T(4,128)S(1)} %get-tuple-element.531), channel_id=1, source_target_pairs={{1,0},{2,1},{3,2},{5,4},{6,5},{7,6},{9,8},{10,9},{11,10},{13,12},{... | collective-permute-start | bytes 23048 | tf_op jit(solution)/shard_map/ppermute | solution.py:26
  98.0 16.1 %collective-permute-start.28 = (f32[64,10,3]{0,2,1:T(4,128)S(1)}, f32[64,10,3]{0,2,1:T(4,128)S(1)}, u32[]{:S(2)}, u32[]{:S(2)}) collective-permute-start(f32[64,10,3]{0,2,1:T(4,128)S(1)} %get-tuple-element.530), channel_id=1, source_target_pairs={{0,1},{1,2},{2,3},{4,5},{5,6},{6,7},{8,9},{9,10},{10,11},{12,13},{... | collective-permute-start | bytes 23048 | tf_op jit(solution)/shard_map/ppermute | solution.py:25
  159.0 13.5 collective-permute-start.37
  160.5 12.1 collective-permute-start.36
  195.4 11.6 collective-permute-start.31
  202.0 11.1 collective-permute-start.45
  299.5 11.4 collective-permute-start.9
  339.1 11.4 collective-permute-start.9
  378.8 11.4 collective-permute-start.9
  418.5 11.4 collective-permute-start.9
  458.1 11.4 collective-permute-start.9
  497.8 11.4 collective-permute-start.9
  537.4 11.4 collective-permute-start.9
  577.1 11.4 collective-permute-start.9
  616.7 11.4 collective-permute-start.9
  656.4 11.4 collective-permute-start.9
  696.0 11.4 collective-permute-start.9
  735.7 11.4 collective-permute-start.9
  775.3 11.4 collective-permute-start.9
  815.0 11.4 collective-permute-start.9
  856.9 16.3 %collective-permute-start.50 = (f32[64,10,1]{2,0,1:T(8,128)}, f32[64,10,1]{2,0,1:T(8,128)}, u32[]{:S(2)}, u32[]{:S(2)}) collective-permute-start(f32[64,10,1]{2,0,1:T(8,128)} %get-tuple-element.529), channel_id=1, source_target_pairs={{0,1},{1,2},{2,3},{4,5},{5,6},{6,7},{8,9},{9,10},{10,11},{12,13},{... | collective-permute-start | bytes 7688 | tf_op jit(solution)/shard_map/ppermute | solution.py:25
  858.2 15.0 collective-permute-start.49
  923.0 17.6 %collective-permute-start.59 = (f32[64,1,128]{2,0,1:T(8,128)S(1)}, f32[64,1,128]{2,0,1:T(8,128)S(1)}, u32[]{:S(2)}, u32[]{:S(2)}) collective-permute-start(f32[64,1,128]{2,0,1:T(8,128)S(1)} %get-tuple-element.553), channel_id=1, source_target_pairs={{4,0},{8,4},{12,8},{5,1},{9,5},{13,9},{6,2},{10,6},{14,10},{7,3},{... | collective-permute-start | bytes 98312 | tf_op jit(solution)/shard_map/ppermute | solution.py:26
  927.6 12.9 collective-permute-start.60
  931.0 71.6 %collective-permute-start.64 = (f32[64,3,64]{0,2,1:T(8,128)}, f32[64,3,64]{0,2,1:T(8,128)}, u32[]{:S(2)}, u32[]{:S(2)}) collective-permute-start(f32[64,3,64]{0,2,1:T(8,128)} %get-tuple-element.585), channel_id=1, source_target_pairs={{4,0},{8,4},{12,8},{5,1},{9,5},{13,9},{6,2},{10,6},{14,10},{7,3},{... | collective-permute-start | bytes 147464 | tf_op jit(solution)/shard_map/ppermute | solution.py:26
  936.2 66.5 %collective-permute-start.63 = (f32[64,3,64]{0,2,1:T(8,128)}, f32[64,3,64]{0,2,1:T(8,128)}, u32[]{:S(2)}, u32[]{:S(2)}) collective-permute-start(f32[64,3,64]{0,2,1:T(8,128)} %get-tuple-element.584), channel_id=1, source_target_pairs={{0,4},{4,8},{8,12},{1,5},{5,9},{9,13},{2,6},{6,10},{10,14},{3,7},{... | collective-permute-start | bytes 147464 | tf_op jit(solution)/shard_map/ppermute | solution.py:25
  965.9 11.3 collective-permute-start.70
  967.4 12.0 collective-permute-start.69
  1048.5 11.1 collective-permute-start.4
  1086.4 11.4 collective-permute-start.4
  1124.0 11.4 collective-permute-start.4
  1161.6 11.4 collective-permute-start.4
  1199.3 11.4 collective-permute-start.4
  1236.9 11.4 collective-permute-start.4
  1274.5 11.4 collective-permute-start.4
  1312.2 11.4 collective-permute-start.4
  1349.8 11.4 collective-permute-start.4
  1387.4 11.4 collective-permute-start.4
  1425.1 11.4 collective-permute-start.4
  1462.7 11.4 collective-permute-start.4
  1500.3 11.4 collective-permute-start.4
  1538.0 11.4 collective-permute-start.4
  1575.6 11.4 collective-permute-start.4
  (430 other events, 3799.5 us)
where the time goes:
time: 1610 us; the launch traced here: 1600 us
  waiting for transfers between devices  702 us (44%)
  starting transfers between devices  504 us (31%)
  local copies, waits for them, and re-layouts  195 us (12%)
  other arithmetic  145 us (9%)
  matrix products  42.4 us (3%)
    ppermute x94, waiting for transfers between devices, padded(): before = lax.ppermute(last, axis, up)  323 us
    ppermute x94, starting transfers between devices, padded(): after = lax.ppermute(first, axis, down)  275 us
    ppermute x31, waiting for transfers between devices, from_behind(): lax.ppermute(value, axis, [(source, source + steps) for source in range(f...  214 us
    ppermute x94, starting transfers between devices, padded(): before = lax.ppermute(last, axis, up)  168 us
    ppermute x94, waiting for transfers between devices, padded(): after = lax.ppermute(first, axis, down)  165 us
    ppermute x31, starting transfers between devices, from_behind(): lax.ppermute(value, axis, [(source, source + steps) for source in range(f...  61.2 us
    dot_general x94, matrix products, column_apply(): jnp.dot(matrix, flattened, precision=lax.Precision.HIGHEST, preferred_ele...  41.2 us
    slice x65, local copies, waits for them, and re-layouts, interior(): volume[:, margin:volume.shape[1] - margin, margin:volume.shape[2] - margin]  38.7 us
  transfers between devices with their start and end apart: 219, of which 166 were waited for; matrix products, arithmetic and copies ran while one was open for 8% of the time, Pallas kernels for 0%

commit v1 on v0

v1 whole, which is shorter than its diff:
```python
import functools
import math

import jax
import jax.numpy as jnp
from jax import lax
from jax.experimental import pallas as pl
from jax.experimental.pallas import tpu as pltpu
from jax.sharding import PartitionSpec as P

F32 = jnp.float32
BF16 = jnp.bfloat16
LATERAL = 0.3
VERTICAL = 4.0
FINE_NODES = [0.0, (1.0 - math.sqrt(3.0 / 7.0)) / 2.0, 0.5, (1.0 + math.sqrt(3.0 / 7.0)) / 2.0, 1.0]
COARSE_NODES = [0.0, 0.5, 1.0]
HALF = 0.5
DEPTH = 64
TX = 8
CXT = 4
FX = 32
GX = 16
LANES = 128
MIB = 2**20


def basis_coeffs(times_list, basis_index):
    coeffs = [1.0]
    denominator = 1.0
    for other_index in range(len(times_list)):
        if other_index != basis_index:
            other_time = times_list[other_index]
            widened = [0.0] * (len(coeffs) + 1)
            for power in range(len(coeffs)):
                widened[power + 1] = widened[power + 1] + coeffs[power]
                widened[power] = widened[power] - other_time * coeffs[power]
            coeffs = widened
            denominator = denominator * (times_list[basis_index] - other_time)
    return [entry / denominator for entry in coeffs]


def poly_value(coeffs, point):
    return sum(coeffs[power] * point**power for power in range(len(coeffs)))


def poly_integral(coeffs, lower, upper):
    return sum(
        coeffs[power] * (upper ** (power + 1) - lower ** (power + 1)) / (power + 1)
        for power in range(len(coeffs))
    )


H = [FINE_NODES[m + 1] - FINE_NODES[m] for m in range(4)]
S = [
    [poly_integral(basis_coeffs(FINE_NODES, j), FINE_NODES[m], FINE_NODES[m + 1]) for j in range(5)]
    for m in range(4)
]
W = [[poly_value(basis_coeffs(COARSE_NODES, c), t) for c in range(3)] for t in FINE_NODES]
SC = [[S[2 * m][j] + S[2 * m + 1][j] for j in range(5)] for m in range(2)]
SW = [[sum(S[m][j] * W[j][c] for j in range(5)) for c in range(3)] for m in range(4)]
ALPHA = [[SW[m][c] - H[m] * W[m][c] for c in range(3)] for m in range(4)]
BETA = [[SW[m][c] - H[m] * W[m + 1][c] for c in range(3)] for m in range(4)]
KE = [[S[m][j] - (H[m] if j == m else 0.0) for j in range(5)] for m in range(4)]
KI = [[S[m][j] - (H[m] if j == m + 1 else 0.0) for j in range(5)] for m in range(4)]


def loop(count, body, unroll=1):
    def step(index, carry):
        body(index)
        return carry

    lax.fori_loop(0, count, step, 0, unroll=unroll)


def roll(value, shift):
    return pltpu.roll(value, shift % value.shape[-1], value.ndim - 1)


def lane(shape):
    return lax.broadcasted_iota(jnp.int32, shape, len(shape) - 1)


def apply4(lhs, value):
    high = value.astype(BF16)
    low = (value - high.astype(F32)).astype(BF16)
    stacked = jnp.concatenate([high, low, high, low], axis=0)
    return jnp.dot(lhs, stacked, preferred_element_type=F32)


def split3(value):
    high = value.astype(BF16)
    rest = value - high.astype(F32)
    mid = rest.astype(BF16)
    low = (rest - mid.astype(F32)).astype(BF16)
    return high, mid, low


def fine_lap(src, row):
    u = src[row + 1]
    even, odd = u[:, :LANES], u[:, LANES:]
    beside = jnp.concatenate([odd + roll(odd, 1), even + roll(even, -1)], axis=1)
    return u, (src[row] + src[row + 2]) + beside - 4.0 * u


def coarse_lap(src, row):
    u = src[row + 1]
    return u, (src[row] + src[row + 2]) + (roll(u, 1) + roll(u, -1)) - 4.0 * u


def pool(first, second):
    total = first + second
    return 0.25 * (total[:, :LANES] + total[:, LANES:])


def twice(value):
    return jnp.concatenate([value, value], axis=1)


def rows8(value):
    return jnp.concatenate([value] * (DEPTH // 8), axis=0)


def zero_edges(ref):
    edge = jnp.zeros(ref.shape[1:], F32)
    ref[0] = edge
    ref[ref.shape[0] - 1] = edge


def coarse_step(src, dst, cc, prop, known=None):
    for pair in range(GX // 2):
        parts = []
        for row in (2 * pair, 2 * pair + 1):
            u, lap = coarse_lap(src, row)
            rhs = u + HALF * (cc[row] * lap)
            parts.append(rhs if known is None else rhs + known[row])
        node = apply4(prop, jnp.concatenate(parts, axis=1))
        dst[2 * pair + 1] = node[:, :LANES]
        dst[2 * pair + 2] = node[:, LANES:]


def chain_power(first, second, cc, prop, steps):
    def body(_):
        coarse_step(first, second, cc, prop)
        coarse_step(second, first, cc, prop)

    loop(steps, body)


def sweep(bufs, cond, lhs, known, ga, uc, saved=None):
    for m in range(4):
        src, dst = bufs[m], bufs[m + 1]
        prop = lhs[0] if m in (0, 3) else lhs[1]

        def body(pair, m=m, src=src, dst=dst, prop=prop):
            us, es, im = [], [], []
            for row in (2 * pair, 2 * pair + 1):
                u, lap = fine_lap(src, row)
                e = cond[row] * lap
                rhs = u + H[m] * e + known(m, row)
                node = apply4(prop, rhs)
                dst[row + 1] = node
                i = (node - rhs) * (1.0 / H[m])
                if saved is not None:
                    saved[0][m, row] = e
                    saved[1][m + 1, row] = i
                us.append(u)
                es.append(e)
                im.append(i)
            e_sum, i_sum = pool(*es), pool(*im)
            for k in range(2):
                value = SC[k][m] * e_sum + SC[k][m + 1] * i_sum
                ga[k, pair] = value if m == 0 else ga[k, pair] + value
            if m in (0, 2):
                uc[m // 2][pair + 1] = pool(*us)

        loop(GX, body, unroll=4)

    def last(pair):
        us, es = [], []
        for row in (2 * pair, 2 * pair + 1):
            u, lap = fine_lap(bufs[4], row)
            us.append(u)
            es.append(cond[row] * lap)
            if saved is not None:
                finish_known(saved, row, es[-1])
        e_sum = pool(*es)
        for k in range(2):
            ga[k, pair] = ga[k, pair] + SC[k][4] * e_sum
        uc[2][pair + 1] = pool(*us)

    loop(GX, last, unroll=2)


def finish_known(saved, row, e_last):
    es, im, k0, plane = saved
    flat = rows8(plane[row])
    values = [es[j, row] for j in range(4)] + [e_last]
    implicit = [im[j, row] for j in range(5)]
    for m in range(4):
        total = H[m] * flat
        for j in range(5):
            total = total + KE[m][j] * values[j] + KI[m][j] * implicit[j]
        k0[m, row] = total


def coarse_known(ga, uc, cc, plane, lhs, kc, k0=None):
    matrix = lhs[3]

    def body(pair):
        rows = (2 * pair, 2 * pair + 1)
        ic, ec = [], []
        for c in range(3):
            laps = [coarse_lap(uc[c], row) for row in rows]
            ec.append([cc[row] * lap for row, (_, lap) in zip(rows, laps)])
            both = apply4(matrix, jnp.concatenate([u for u, _ in laps], axis=1))
            ic.append([both[:, :LANES], both[:, LANES:]])
        for place, row in enumerate(rows):
            flat = rows8(plane[row])
            for k in range(2):
                kc[k, row] = (
                    (ga[k, row] + SC[k][0] * ic[0][place])
                    + HALF * flat
                    - HALF * (ec[k][place] + ic[k + 1][place])
                )
            if k0 is not None:
                for m in range(4):
                    total = ALPHA[m][0] * ec[0][place] + BETA[m][0] * ic[0][place]
                    for c in (1, 2):
                        total = total + ALPHA[m][c] * ec[c][place] + BETA[m][c] * ic[c][place]
                    wide = twice(total)
                    k0[m, 2 * row] = k0[m, 2 * row] - wide
                    k0[m, 2 * row + 1] = k0[m, 2 * row + 1] - wide

    loop(GX // 2, body, unroll=2)


def pack(c_ref, base, main, to_right, to_left):
    rows = [c_ref[base + r] for r in range(CXT)]
    at = lane((DEPTH, LANES))
    for half in range(2):
        main[half] = jnp.where(at < 64, roll(rows[2 * half], -32), roll(rows[2 * half + 1], 32))
    for out, start in ((to_right, 64), (to_left, 32)):
        value = roll(rows[0], -start)
        for r in range(1, CXT):
            value = jnp.where(at < 32 * r, value, roll(rows[r], 32 * r - start))
        out[0] = value


def unpack(got, dst):
    at = lane((DEPTH, LANES))
    for g in range(GX // CXT):
        for r in range(CXT):
            centre = roll(got[g, r // 2], 32 if r % 2 == 0 else -32)
            left = roll(got[g, 2], -32 * r)
            right = roll(got[g, 3], 96 - 32 * r)
            value = jnp.where(at < 32, left, jnp.where(at < 96, centre, right))
            dst[CXT * g + r + 1] = value


def props_kernel(upper_ref, lower_ref, out_ref):
    upper, lower = upper_ref[...], lower_ref[...]
    shape = (DEPTH, LANES)
    row = lax.broadcasted_iota(jnp.int32, shape, 0)
    col = lane(shape)
    level = jnp.where(col < DEPTH, col, col - DEPTH)
    eye = jnp.where(row == level, 1.0, 0.0).astype(F32)

    def shifted(value, step):
        return pltpu.roll(value, step % DEPTH, 0)

    def inverse(length):
        a = -VERTICAL * length * jnp.where(row == 0, 0.0, upper)
        c = -VERTICAL * length * lower
        b = 1.0 + VERTICAL * length * (upper + lower)
        r = eye
        step = 1
        while step < DEPTH:
            alpha = -a / shifted(b, step)
            gamma = -c / shifted(b, -step)
            b, r, a, c = (
                b + alpha * shifted(c, step) + gamma * shifted(a, -step),
                r + alpha * shifted(r, step) + gamma * shifted(r, -step),
                alpha * shifted(a, step),
                gamma * shifted(c, -step),
            )
            step *= 2
        return r / b

    def store(index, value):
        high = value.astype(BF16)
        out_ref[index, :, :LANES] = high
        out_ref[index, :, LANES:] = (value - high.astype(F32)).astype(BF16)

    fine = inverse(jnp.where(col < DEPTH, H[0], H[1]).astype(F32))
    other = roll(fine, DEPTH)
    store(0, jnp.where(col < DEPTH, fine, other))
    store(1, jnp.where(col < DEPTH, other, fine))
    store(2, inverse(jnp.full(shape, HALF, F32)))
    matrix = jnp.where(row == level, -VERTICAL * (upper + lower), 0.0)
    matrix = matrix + jnp.where(level == row - 1, VERTICAL * upper, 0.0)
    matrix = matrix + jnp.where(level == row + 1, VERTICAL * lower, 0.0)
    store(3, matrix)


def prep_kernel(field_ref, count_ref, main, to_right, to_left):
    src = lax.broadcasted_iota(jnp.int32, (LANES, LANES), 0)
    dst = lane((LANES, LANES))
    target = jnp.where(dst < 64, 2 * dst, 2 * (dst - 64) + 1)
    pick = jnp.where(src == target, 1.0, 0.0).astype(BF16)
    for row in range(TX):
        main[row, : 2 * DEPTH] = sum(
            jnp.dot(part, pick, preferred_element_type=F32) for part in split3(field_ref[row])
        )
    counts = count_ref[...].reshape(TX * 8, LANES).astype(BF16)
    counts = jnp.dot(counts, pick, preferred_element_type=F32)
    for row in range(TX):
        main[row, 2 * DEPTH :] = counts[8 * row : 8 * row + 8]
    at = lane((2 * DEPTH + 8, LANES))
    for slab in range(TX // 2):
        low, high = main[slab], main[slab + TX // 2]
        to_right[slab] = jnp.where(
            at < 64,
            jnp.where(at < 32, roll(low, -32), roll(low, -64)),
            jnp.where(at < 96, roll(high, 32), high),
        )
        to_left[slab] = jnp.where(
            at < 64,
            jnp.where(at < 32, low, roll(low, -32)),
            jnp.where(at < 96, roll(high, 64), roll(high, 32)),
        )


def first_kernel(
    flags,
    place,
    main,
    strip,
    tables,
    lhs,
    c_out,
    hop,
    k0,
    v_out,
    kc_out,
    cc,
    cond,
    plane_c,
    init,
    buf_a,
    buf_b,
    planes,
    es,
    im,
    uc0,
    uc1,
    uc2,
    ga,
    kc,
    node_a,
    node_b,
    planes_c,
):
    for ref in (init, buf_a, buf_b, uc0, uc1, uc2, node_a, node_b):
        zero_edges(ref)
    at = lane((2 * DEPTH + 8, LANES))

    def assemble(g):
        for q in range(TX):
            row = TX * g + q
            centre = main[g, q]
            left, right = strip[g, q % 4], strip[g, 4 + q % 4]
            off = 64 * (q // 4)
            halves = []
            for odd in range(2):
                a = roll(left, -(off + 32 * odd))
                b = roll(centre, 32 if odd == 0 else -32)
                c = roll(right, 96 - off - 32 * odd)
                halves.append(jnp.where(at < 32, a, jnp.where(at < 96, b, c)))
            window = jnp.concatenate(halves, axis=1)
            init[row + 1] = window[:DEPTH]
            cond[row] = LATERAL * window[DEPTH : 2 * DEPTH]
            counts = window[2 * DEPTH :]
            for t in range(3):
                rate = jnp.concatenate([tables[t], tables[t]], axis=1)
                heat = jnp.sum(counts * rate, axis=0, keepdims=True)
                planes[t, row] = jnp.broadcast_to(heat, (8, 2 * LANES))

    loop(FX // TX, assemble)

    def coarsen(row):
        cc[row] = 0.25 * pool(cond[2 * row], cond[2 * row + 1])
        for t in range(3):
            planes_c[t, row] = pool(planes[t, 2 * row], planes[t, 2 * row + 1])

    loop(GX, coarsen, unroll=4)
    uc = (uc0, uc1, uc2)
    bufs = (init, buf_a, buf_b, buf_a, buf_b)
    prop = lhs[2]

    def start_from_zero():
        def body(pair):
            both = apply4(prop, jnp.concatenate([kc[0, 2 * pair], kc[0, 2 * pair + 1]], axis=1))
            node_b[2 * pair + 1] = both[:, :LANES]
            node_b[2 * pair + 2] = both[:, LANES:]

        loop(GX // 2, body, unroll=4)
        coarse_step(node_b, node_a, cc, prop, kc.at[1])

    def heat(t):
        return lambda m, row: H[m] * rows8(planes[t, row])

    sweep(bufs, cond, lhs, heat(2), ga, uc)
    coarse_known(ga, uc, cc, planes_c.at[2], lhs, kc)
    start_from_zero()
    after1, after2, is1, is0 = flags[0], flags[1], flags[2], flags[3]

    def choose2(row):
        node_a[row + 1] = after2 * node_a[row + 1] + is1 * uc0[row + 1]

    loop(GX, choose2, unroll=4)
    chain_power(node_a, node_b, cc, prop, 1)

    def keep(row):
        c_out[row] = node_a[row + 1]

    loop(GX, keep, unroll=4)
    sweep(bufs, cond, lhs, heat(1), ga, uc)
    coarse_known(ga, uc, cc, planes_c.at[1], lhs, kc)
    start_from_zero()

    def choose1(row):
        c_out[row] = c_out[row] + (after1 * node_a[row + 1] + is0 * uc0[row + 1])
        for fine in (2 * row, 2 * row + 1):
            before = buf_b[fine + 1] - twice(uc2[row + 1])
            here = init[fine + 1] - twice(uc0[row + 1])
            v_out[fine] = after1 * before + is0 * here

    loop(GX, choose1, unroll=2)
    for r in range(CXT):
        hop[r] = c_out[place[0] * CXT + r]

    def implicit_zero(row):
        im[0, row] = apply4(lhs[3], init[row + 1])

    loop(FX, implicit_zero, unroll=4)
    sweep(bufs, cond, lhs, heat(0), ga, uc, saved=(es, im, k0, planes.at[0]))
    coarse_known(ga, uc, cc, planes_c.at[0], lhs, kc_out, k0)

    def keep_plane(row):
        plane_c[row] = planes_c[0, row]

    loop(GX, keep_plane, unroll=4)


def phase_kernel(
    steps, strips_in, strips_out, place, got, c_in, cc, lhs, c_out, *rest
):
    node_a, node_b = rest[-2:]
    outs = rest[:-2]
    zero_edges(node_a)
    zero_edges(node_b)
    if strips_in:
        unpack(got, node_a)
    else:

        def load(row):
            node_a[row + 1] = got[row]

        loop(GX, load, unroll=4)
    chain_power(node_a, node_b, cc, lhs[2], steps)

    def add(row):
        c_out[row] = c_in[row] + node_a[row + 1]

    loop(GX, add, unroll=4)
    base = place[0] * CXT
    if strips_out:
        pack(c_out, base, *outs)
    else:
        for r in range(CXT):
            outs[0][r] = c_out[base + r]


def second_kernel(
    steps,
    flags,
    place,
    got,
    c_in,
    cc,
    lhs,
    k0,
    v,
    kc_in,
    cond,
    plane_c,
    c_out,
    hop,
    v_tile,
    start,
    buf_a,
    buf_b,
    dk,
    uc0,
    uc1,
    uc2,
    ga,
    kc,
    node_a,
    node_b,
    node_c,
):
    for ref in (start, buf_a, buf_b, uc0, uc1, uc2, node_a, node_b, node_c):
        zero_edges(ref)
    unpack(got, node_a)
    prop, matrix = lhs[2], lhs[3]
    chain_power(node_a, node_b, cc, prop, steps)

    def add(row):
        value = c_in[row] + node_a[row + 1]
        node_a[row + 1] = value
        wide = twice(value)
        start[2 * row + 1] = v[2 * row] + wide
        start[2 * row + 2] = v[2 * row + 1] + wide

    loop(GX, add, unroll=4)

    def spread(row, c, explicit, implicit, first):
        for m in range(4):
            total = ALPHA[m][c] * explicit + BETA[m][c] * implicit
            dk[m, row] = total if first else dk[m, row] + total

    def stage(c, src, dst):
        def body(pair):
            rows = (2 * pair, 2 * pair + 1)
            laps = [coarse_lap(src, row) for row in rows]
            ex = [cc[row] * lap for row, (_, lap) in zip(rows, laps)]
            if c == 0:
                both = apply4(matrix, jnp.concatenate([u for u, _ in laps], axis=1))
                spread(rows[0], 0, ex[0], both[:, :LANES], True)
                spread(rows[1], 0, ex[1], both[:, LANES:], True)
            else:
                spread(rows[0], c, ex[0], kc[c - 1, rows[0]], False)
                spread(rows[1], c, ex[1], kc[c - 1, rows[1]], False)
            if c < 2:
                rhs = jnp.concatenate(
                    [u + HALF * e + kc_in[c, row] for row, (u, _), e in zip(rows, laps, ex)],
                    axis=1,
                )
                node = apply4(prop, rhs)
                dst[rows[0] + 1] = node[:, :LANES]
                dst[rows[1] + 1] = node[:, LANES:]
                implicit = (node - rhs) * (1.0 / HALF)
                kc[c, rows[0]] = implicit[:, :LANES]
                kc[c, rows[1]] = implicit[:, LANES:]

        loop(GX // 2, body, unroll=2)

    stage(0, node_a, node_b)
    stage(1, node_b, node_c)
    stage(2, node_c, None)

    def known(m, row):
        return k0[m, row] + twice(dk[m, row // 2])

    uc = (uc0, uc1, uc2)
    sweep((start, buf_a, buf_b, buf_a, buf_b), cond, lhs, known, ga, uc)
    coarse_known(ga, uc, cc, plane_c, lhs, kc)
    is0 = flags[3]

    def begin(row):
        node_a[row + 1] = is0 * uc0[row + 1]

    loop(GX, begin, unroll=4)
    coarse_step(node_a, node_b, cc, prop, kc.at[0])
    coarse_step(node_b, node_a, cc, prop, kc.at[1])

    def keep(row):
        c_out[row] = node_a[row + 1]

    loop(GX, keep, unroll=4)
    base = place[0] * CXT
    for r in range(CXT):
        hop[r] = c_out[base + r]
        for q in range(2):
            fine = 2 * r + q
            v_tile[fine] = buf_b[2 * base + fine + 1] - twice(uc2[base + r + 1])


def last_kernel(steps, place, got, c_in, cc, lhs, v_tile, out, node_a, node_b):
    zero_edges(node_a)
    zero_edges(node_b)
    unpack(got, node_a)
    chain_power(node_a, node_b, cc, lhs[2], steps)
    base = place[0] * CXT
    src = lax.broadcasted_iota(jnp.int32, (2 * LANES, LANES), 0)
    dst = lane((2 * LANES, LANES))
    target = 32 + dst // 2 + jnp.where(dst % 2 == 1, LANES, 0)
    pick = jnp.where(src == target, 1.0, 0.0).astype(BF16)
    for r in range(CXT):
        wide = twice(c_in[base + r] + node_a[base + r + 1])
        for q in range(2):
            value = v_tile[2 * r + q] + wide
            out[2 * r + q] = sum(
                jnp.dot(part, pick, preferred_element_type=F32) for part in split3(value)
            )


VMEM = pl.BlockSpec(memory_space=pltpu.VMEM)
SMEM = pl.BlockSpec(memory_space=pltpu.SMEM)


def shape(*dims, dtype=F32):
    return jax.ShapeDtypeStruct(dims, dtype)


def call(kernel, name, outs, scratch, smem, *operands, limit=40, flops=10**8):
    return pl.pallas_call(
        kernel,
        name=name,
        out_shape=outs,
        in_specs=[SMEM] * smem + [VMEM] * (len(operands) - smem),
        out_specs=jax.tree.map(lambda _: VMEM, outs),
        scratch_shapes=[pltpu.VMEM(dims, F32) for dims in scratch],
        compiler_params=pltpu.CompilerParams(vmem_limit_bytes=limit * MIB),
        cost_estimate=pl.CostEstimate(flops=flops, bytes_accessed=10**6, transcendentals=0),
    )(*operands)


COARSE = (GX, DEPTH, LANES)
COARSE_PAD = (GX + 2, DEPTH, LANES)
FINE = (FX, DEPTH, 2 * LANES)
FINE_PAD = (FX + 2, DEPTH, 2 * LANES)
HOP = (CXT, DEPTH, LANES)


def shift(value, steps, sideways=0):
    slices, columns = lax.axis_size("tm"), lax.axis_size("gy")
    pairs = [
        (s * columns + g, (s + steps) * columns + g + sideways)
        for s in range(slices - steps)
        for g in range(columns)
        if 0 <= g + sideways < columns
    ]
    return lax.ppermute(value, ("tm", "gy"), pairs)


def fetch_plain(hop, steps):
    return lax.all_gather(shift(hop, steps), "gx").reshape(COARSE)


def fetch_strips(main, to_right, to_left, steps):
    parts = [shift(main, steps), shift(to_right, steps, 1), shift(to_left, steps, -1)]
    return lax.all_gather(jnp.concatenate(parts, axis=0), "gx")


def on_device(initial_temp, conductivity, vert_cond, borehole_cells, borehole_profiles, heat_table):
    slice_index = lax.axis_index("tm")
    place = lax.axis_index("gx").astype(jnp.int32).reshape(1)
    flags = jnp.stack(
        [slice_index >= 1, slice_index >= 2, slice_index == 1, slice_index == 0]
    ).astype(F32)
    profiles = heat_table.shape[0]
    tables = jnp.stack([heat_table, shift(heat_table, 1), shift(heat_table, 2)])
    tables = jnp.broadcast_to(tables, (3, profiles, LANES))
    cells = borehole_cells.reshape(-1)
    which = borehole_profiles.reshape(-1)
    at_cell = cells[:, None, None, None] == (
        jnp.arange(TX)[:, None, None] * LANES + jnp.arange(LANES)[None, None, :]
    )
    at_profile = which[:, None, None, None] == jnp.arange(profiles)[None, :, None]
    counts = jnp.sum((at_cell & at_profile).astype(F32), axis=0)

    fields = jnp.transpose(jnp.concatenate([initial_temp, conductivity], axis=0), (1, 0, 2))
    main, to_right, to_left = call(
        prep_kernel,
        "prep",
        [
            shape(TX, 2 * DEPTH + 8, LANES),
            shape(TX // 2, 2 * DEPTH + 8, LANES),
            shape(TX // 2, 2 * DEPTH + 8, LANES),
        ],
        [],
        0,
        fields,
        counts,
    )
    strip = jnp.concatenate([shift(to_right, 0, 1), shift(to_left, 0, -1)], axis=0)
    main = lax.all_gather(main, "gx")
    strip = lax.all_gather(strip, "gx")
    upper = jnp.broadcast_to(vert_cond[:, None], (DEPTH, LANES))
    lower = jnp.concatenate([vert_cond[1:], jnp.zeros((1,), F32)])
    lower = jnp.broadcast_to(lower[:, None], (DEPTH, LANES))
    lhs = call(
        props_kernel, "props", shape(4, DEPTH, 2 * LANES, dtype=BF16), [], 0, upper, lower
    )

    c, hop, k0, v, kc, cc, cond, plane_c = call(
        first_kernel,
        "first_sweeps",
        [
            shape(*COARSE),
            shape(*HOP),
            shape(4, *FINE),
            shape(*FINE),
            shape(2, *COARSE),
            shape(*COARSE),
            shape(*FINE),
            shape(GX, 8, LANES),
        ],
        [
            FINE_PAD,
            FINE_PAD,
            FINE_PAD,
            (3, FX, 8, 2 * LANES),
            (4, *FINE),
            (5, *FINE),
            COARSE_PAD,
            COARSE_PAD,
            COARSE_PAD,
            (2, *COARSE),
            (2, *COARSE),
            COARSE_PAD,
            COARSE_PAD,
            (3, GX, 8, LANES),
        ],
        2,
        flags,
        place,
        main,
        strip,
        tables,
        lhs,
        limit=60,
    )

    packed = [shape(2, DEPTH, LANES), shape(1, DEPTH, LANES), shape(1, DEPTH, LANES)]

    def phase(steps, name, got, c, strips_in, strips_out):
        outs = [shape(*COARSE)] + (packed if strips_out else [shape(*HOP)])
        kernel = functools.partial(phase_kernel, steps, strips_in, strips_out)
        c, *hops = call(
            kernel, name, outs, [COARSE_PAD, COARSE_PAD], 1, place, got, c, cc, lhs
        )
        return c, hops

    c, (hop,) = phase(2, "chain_a2", fetch_plain(hop, 2), c, False, False)
    c, hops = phase(4, "chain_a4", fetch_plain(hop, 4), c, False, True)
    got = fetch_strips(*hops, 8)
    c, hop, v_tile = call(
        functools.partial(second_kernel, 8),
        "second_sweep",
        [shape(*COARSE), shape(*HOP), shape(TX, DEPTH, 2 * LANES)],
        [
            FINE_PAD,
            FINE_PAD,
            FINE_PAD,
            (4, *COARSE),
            COARSE_PAD,
            COARSE_PAD,
            COARSE_PAD,
            (2, *COARSE),
            (2, *COARSE),
            COARSE_PAD,
            COARSE_PAD,
            COARSE_PAD,
        ],
        2,
        flags,
        place,
        got,
        c,
        cc,
        lhs,
        k0,
        v,
        kc,
        cond,
        plane_c,
        limit=60,
    )
    c, (hop,) = phase(1, "chain_b1", fetch_plain(hop, 1), c, False, False)
    c, hops = phase(2, "chain_b2", fetch_plain(hop, 2), c, False, True)
    c, hops = phase(4, "chain_b4", fetch_strips(*hops, 4), c, True, True)
    out = call(
        functools.partial(last_kernel, 8),
        "finish",
        shape(TX, DEPTH, LANES),
        [COARSE_PAD, COARSE_PAD],
        1,
        place,
        fetch_strips(*hops, 8),
        c,
        cc,
        lhs,
        v_tile,
    )
    return jnp.transpose(out, (1, 0, 2))[None]


def solution(mesh):
    placed = (
        P(None, "gx", "gy"),
        P(None, "gx", "gy"),
        P(),
        P("gx", "gy", None),
        P("gx", "gy", None),
        P(None, "tm"),
    )
    return jax.shard_map(
        on_device, mesh=mesh, in_specs=placed, out_specs=P("tm", None, "gx", "gy"), check_vma=False
    )
```

time: 1610 us -> 334 us (0.21)
  waiting for transfers between devices: 702 us -> 95.2 us
  starting transfers between devices: 504 us -> 45.8 us
  local copies, waits for them, and re-layouts: 195 us -> 7.57 us
  other arithmetic: 145 us -> 3.36 us
  Pallas kernels: 0 us -> 105 us
  blocking collectives: 0 us -> 58 us
  matrix products: 42.4 us -> 0 us
    ppermute x219 -> x17, waiting for transfers between devices: 702 us -> 58 us  [shift(): return lax.ppermute(value, ('tm', 'gy'), pairs)]
    ppermute x219 -> x17, starting transfers between devices: 504 us -> 45.8 us  [shift(): return lax.ppermute(value, ('tm', 'gy'), pairs)]
    pallas_call x0 -> x10, Pallas kernels: none -> 105 us  [call(): pl.pallas_call(kernel, name=name, out_shape=outs, in_specs=[SMEM] * smem...]
    slice x151 -> x1, local copies, waits for them, and re-layouts: 77.8 us -> 0.07 us  [on_device(): lower = jnp.concatenate([vert_cond[1:], jnp.zeros((1,), F32)])]
    all_gather x0 -> x7, blocking collectives: none -> 58 us  [the longest x4 33.4 us: fetch_plain(): return lax.all_gather(shift(hop, steps), 'gx').reshape(COARSE)]
    reshape x174 -> x0, local copies, waits for them, and re-layouts: 53 us -> none  [the longest x79 33.5 us: column_apply(): return product.reshape(volume.shape)]
    dot_general x94 -> x0, matrix products: 41.2 us -> none  [column_apply(): jnp.dot(matrix, flattened, precision=lax.Precision.HIGHEST, preferred_ele...]
    add x83 -> x1, other arithmetic: 40.3 us -> 0.07 us  [on_device(): jnp.arange(TX)[:, None, None] * LANES + jnp.arange(LANES)[None, None, :]]
  transfers between devices with their start and end apart: 219 -> 19, of which waited for: 166 -> 12; matrix products, arithmetic and copies ran while one was open for 8% -> 1% of each run, Pallas kernels for 0% -> 0%
where the time goes in v1:
time: 334 us; the launch traced here: 329 us
  Pallas kernels  105 us (31%)
  waiting for transfers between devices  95.2 us (29%)
  blocking collectives  58 us (17%)
  starting transfers between devices  45.8 us (14%)
  between operations  13.7 us (4%)
  local copies, waits for them, and re-layouts  7.57 us (2%)
  other arithmetic  3.36 us (1%)
    pallas_call x10, Pallas kernels, call(): pl.pallas_call(kernel, name=name, out_shape=outs, in_specs=[SMEM] * smem...  105 us
    ppermute x17, waiting for transfers between devices, shift(): return lax.ppermute(value, ('tm', 'gy'), pairs)  58 us
    ppermute x17, starting transfers between devices, shift(): return lax.ppermute(value, ('tm', 'gy'), pairs)  45.8 us
    all_gather x4, blocking collectives, fetch_plain(): return lax.all_gather(shift(hop, steps), 'gx').reshape(COARSE)  33.4 us
    all_gather x1, waiting for transfers between devices, on_device(): strip = lax.all_gather(strip, 'gx')  31.2 us
    all_gather x3, blocking collectives, fetch_strips(): return lax.all_gather(jnp.concatenate(parts, axis=0), 'gx')  24.6 us
  transfers between devices with their start and end apart: 19, of which 12 were waited for; matrix products, arithmetic and copies ran while one was open for 1% of the time, Pallas kernels for 0%

profile of v1, /device:TPU:30, one launch (start us, length us, event | category | flops | bytes accessed | tf_op | source)
XLA Modules:
  0.0 329.0 jit_solution(5021164921320440580)
XLA Ops:
  7.3 1.0 copy.13
  8.4 1.0 copy.14
  10.3 1.2 prep.1
  11.6 1.3 collective-permute-start
  12.9 4.6 %collective-permute-start.1 = (f32[4,136,128]{2,1,0:T(8,128)S(1)}, f32[4,136,128]{2,1,0:T(8,128)S(1)}, u32[]{:S(2)}, u32[]{:S(2)}) collective-permute-start(f32[4,136,128]{2,1,0:T(8,128)S(1)} %get-tuple-element.37), channel_id=1, source_target_pairs={{1,0},{2,1},{3,2},{17,16},{18,17},{19,18},{33,32},{34,33},{35,34},... | collective-permute-start | bytes 835592 | tf_op jit(solution)/shard_map/ppermute | solution.py:645
  17.5 4.4 %collective-permute-done = f32[4,136,128]{2,1,0:T(8,128)S(1)} collective-permute-done((f32[4,136,128]{2,1,0:T(8,128)S(1)}, f32[4,136,128]{2,1,0:T(8,128)S(1)}, u32[]{:S(2)}, u32[]{:S(2)}) %collective-permute-start) | collective-permute-done | bytes 278560 | tf_op jit(solution)/shard_map/ppermute | solution.py:645
  21.9 1.2 collective-permute-done.1
  24.0 5.2 %collective-permute-start.3 = (f32[8,1]{0,1:T(1,128)S(1)}, f32[8,1]{0,1:T(1,128)S(1)}, u32[]{:S(2)}, u32[]{:S(2)}) collective-permute-start(f32[8,1]{0,1:T(1,128)S(1)} %copy-done.11), channel_id=1, source_target_pairs={{0,32},{1,33},{2,34},{3,35},{16,48},{17,49},{18,50},{19,51},{32,64... | collective-permute-start | bytes 104 | tf_op jit(solution)/shard_map/ppermute | solution.py:645
  29.2 3.8 %collective-permute-start.2 = (f32[8,1]{0,1:T(1,128)S(1)}, f32[8,1]{0,1:T(1,128)S(1)}, u32[]{:S(2)}, u32[]{:S(2)}) collective-permute-start(f32[8,1]{0,1:T(1,128)S(1)} %copy-done.11), channel_id=1, source_target_pairs={{0,16},{1,17},{2,18},{3,19},{16,32},{17,33},{18,34},{19,35},{32,48... | collective-permute-start | bytes 104 | tf_op jit(solution)/shard_map/ppermute | solution.py:645
  35.0 1.7 collective-permute-done.2
  36.7 6.0 %all-gather.12.cloned.1.call-done = f32[32,136,128]{2,1,0:T(8,128)} async-done(((f32[8,136,128]{2,1,0:T(8,128)}), f32[32,136,128]{2,1,0:T(8,128)}) %all-gather.12.cloned.1.call-update) | async-done | bytes 2228240 | tf_op jit(solution)/shard_map/all_gather | solution.py:689
  42.7 31.2 %all-gather.14.cloned.1.call-done = f32[32,136,128]{2,1,0:T(8,128)} async-done(((f32[8,136,128]{2,1,0:T(8,128)}), f32[32,136,128]{2,1,0:T(8,128)}) %all-gather.14.cloned.1.call-update) | async-done | bytes 2228240 | tf_op jit(solution)/shard_map/all_gather | solution.py:690
  74.6 54.4 %first_sweeps.1 = (f32[16,64,128]{2,1,0:T(8,128)}, f32[4,64,128]{2,1,0:T(8,128)}, f32[4,32,64,256]{3,2,1,0:T(8,128)}, f32[32,64,256]{2,1,0:T(8,128)}, f32[2,16,6...) custom-call(f32[4]{0:T(128)} %add_convert_fusion.flags, ...), custom_call_target="tpu_custom_call" | custom-call | flops 100000000 | bytes 1000000 | tf_op jit(solution)/shard_map/first_sweeps/pallas_call | solution.py:618
  128.9 4.6 %collective-permute-start.4 = (f32[4,64,128]{2,1,0:T(8,128)}, f32[4,64,128]{2,1,0:T(8,128)S(1)}, u32[]{:S(2)}, u32[]{:S(2)}) collective-permute-start(f32[4,64,128]{2,1,0:T(8,128)} %get-tuple-element.38), channel_id=1, source_target_pairs={{0,32},{1,33},{2,34},{3,35},{16,48},{17,49},{18,50},{19,51},{32,64... | collective-permute-start | bytes 393224 | tf_op jit(solution)/shard_map/ppermute | solution.py:645
  133.5 8.2 %collective-permute-done.4 = f32[4,64,128]{2,1,0:T(8,128)S(1)} collective-permute-done((f32[4,64,128]{2,1,0:T(8,128)}, f32[4,64,128]{2,1,0:T(8,128)S(1)}, u32[]{:S(2)}, u32[]{:S(2)}) %collective-permute-start.4) | collective-permute-done | bytes 131104 | tf_op jit(solution)/shard_map/ppermute | solution.py:645
  141.8 8.5 %all-gather.2.got = f32[16,64,128]{2,1,0:T(8,128)S(1)} all-gather(f32[4,64,128]{2,1,0:T(8,128)S(1)} %collective-permute-done.4), channel_id=4, replica_groups=mesh['tm'=16,'gx'=4,'gy'=4] {'gx'}, dimensions={0}, use_global_device_ids=true | all-gather | bytes 655360 | tf_op jit(solution)/shard_map/all_gather | solution.py:649
  150.3 1.0 copy-done
  151.3 1.0 copy-done.7
  152.4 1.9 chain_a2.1
  154.3 7.2 %collective-permute-start.5 = (f32[4,64,128]{2,1,0:T(8,128)S(1)}, f32[4,64,128]{2,1,0:T(8,128)S(1)}, u32[]{:S(2)}, u32[]{:S(2)}) collective-permute-start(f32[4,64,128]{2,1,0:T(8,128)S(1)} %get-tuple-element.41), channel_id=1, source_target_pairs={{0,64},{1,65},{2,66},{3,67},{16,80},{17,81},{18,82},{19,83},{32,96... | collective-permute-start | bytes 393224 | tf_op jit(solution)/shard_map/ppermute | solution.py:645
  161.5 7.5 %collective-permute-done.5 = f32[4,64,128]{2,1,0:T(8,128)S(1)} collective-permute-done((f32[4,64,128]{2,1,0:T(8,128)S(1)}, f32[4,64,128]{2,1,0:T(8,128)S(1)}, u32[]{:S(2)}, u32[]{:S(2)}) %collective-permute-start.5) | collective-permute-done | bytes 131104 | tf_op jit(solution)/shard_map/ppermute | solution.py:645
  169.0 8.5 %all-gather.3.got = f32[16,64,128]{2,1,0:T(8,128)S(1)} all-gather(f32[4,64,128]{2,1,0:T(8,128)S(1)} %collective-permute-done.5), channel_id=5, replica_groups=mesh['tm'=16,'gx'=4,'gy'=4] {'gx'}, dimensions={0}, use_global_device_ids=true | all-gather | bytes 655360 | tf_op jit(solution)/shard_map/all_gather | solution.py:649
  177.5 3.7 %chain_a4.1 = (f32[16,64,128]{2,1,0:T(8,128)S(1)}, f32[2,64,128]{2,1,0:T(8,128)S(1)}, f32[1,64,128]{2,1,0:T(8,128)S(1)}, f32[1,64,128]{2,1,0:T(8,128)S(1)}) custom-call(s32[1]{0:T(128)} %bitcast.place, f32[16,64,128]{2,1,0:T(8,128)S(1)} %all-gather.3.got, f32[16,64,128]{2,1,0:T(8,128)S(1)} %get-tuple-element.42.c_in, f32[16,64,128]{2,1,0:T(8,128)S(1)} %copy-done.1, ...), custom_call_target="tpu_custom_call" | custom-call | flops 100000000 | bytes 1000000 | tf_op jit(solution)/shard_map/chain_a4/pallas_call | solution.py:618
  181.2 1.3 collective-permute-start.6
  182.5 1.3 collective-permute-start.7
  184.5 4.7 %collective-permute-done.7 = f32[1,64,128]{2,1,0:T(8,128)S(1)} collective-permute-done((f32[1,64,128]{2,1,0:T(8,128)S(1)}, f32[1,64,128]{2,1,0:T(8,128)S(1)}, u32[]{:S(2)}, u32[]{:S(2)}) %collective-permute-start.7) | collective-permute-done | bytes 32800 | tf_op jit(solution)/shard_map/ppermute | solution.py:645
  189.2 8.5 %all-gather.4 = f32[16,64,128]{2,1,0:T(8,128)} all-gather(f32[4,64,128]{2,1,0:T(8,128)S(1)} %pad_maximum_fusion.1), channel_id=6, replica_groups=mesh['tm'=16,'gx'=4,'gy'=4] {'gx'}, dimensions={0}, use_global_device_ids=true | all-gather | bytes 655360 | tf_op jit(solution)/shard_map/all_gather | solution.py:654
  197.7 29.1 %second_sweep.1 = (f32[16,64,128]{2,1,0:T(8,128)}, f32[4,64,128]{2,1,0:T(8,128)}, f32[8,64,256]{2,1,0:T(8,128)}) custom-call(f32[4]{0:T(128)} %add_convert_fusion.flags, s32[1]{0:T(128)} %bitcast.place, f32[4,4,64,128]{3,2,1,0:T(8,128)} %bitcast.28, f32[16,64,128]{2,1,0:T(8,128)} %copy-done.6, f32[16,64,128]{2,1,0:T(8,128)} %get-tuple-element.40.cc, ...), custom_call_target="tpu_custom_call" | custom-call | flops 100000000 | bytes 1000000 | tf_op jit(solution)/shard_map/second_sweep/pallas_call | solution.py:618
  226.8 4.5 %collective-permute-start.9 = (f32[4,64,128]{2,1,0:T(8,128)}, f32[4,64,128]{2,1,0:T(8,128)S(1)}, u32[]{:S(2)}, u32[]{:S(2)}) collective-permute-start(f32[4,64,128]{2,1,0:T(8,128)} %get-tuple-element.52), channel_id=1, source_target_pairs={{0,16},{1,17},{2,18},{3,19},{16,32},{17,33},{18,34},{19,35},{32,48... | collective-permute-start | bytes 393224 | tf_op jit(solution)/shard_map/ppermute | solution.py:645
  231.3 5.4 %collective-permute-done.9 = f32[4,64,128]{2,1,0:T(8,128)S(1)} collective-permute-done((f32[4,64,128]{2,1,0:T(8,128)}, f32[4,64,128]{2,1,0:T(8,128)S(1)}, u32[]{:S(2)}, u32[]{:S(2)}) %collective-permute-start.9) | collective-permute-done | bytes 131104 | tf_op jit(solution)/shard_map/ppermute | solution.py:645
  236.7 8.0 %all-gather.5.got = f32[16,64,128]{2,1,0:T(8,128)S(1)} all-gather(f32[4,64,128]{2,1,0:T(8,128)S(1)} %collective-permute-done.9), channel_id=7, replica_groups=mesh['tm'=16,'gx'=4,'gy'=4] {'gx'}, dimensions={0}, use_global_device_ids=true | all-gather | bytes 655360 | tf_op jit(solution)/shard_map/all_gather | solution.py:649
  244.7 1.0 copy-done.8
  245.8 1.0 chain_b1.1
  246.7 2.4 collective-permute-start.10
  249.1 10.2 %collective-permute-done.10 = f32[4,64,128]{2,1,0:T(8,128)S(1)} collective-permute-done((f32[4,64,128]{2,1,0:T(8,128)S(1)}, f32[4,64,128]{2,1,0:T(8,128)S(1)}, u32[]{:S(2)}, u32[]{:S(2)}) %collective-permute-start.10) | collective-permute-done | bytes 131104 | tf_op jit(solution)/shard_map/ppermute | solution.py:645
  259.3 8.4 %all-gather.6.got = f32[16,64,128]{2,1,0:T(8,128)S(1)} all-gather(f32[4,64,128]{2,1,0:T(8,128)S(1)} %collective-permute-done.10), channel_id=8, replica_groups=mesh['tm'=16,'gx'=4,'gy'=4] {'gx'}, dimensions={0}, use_global_device_ids=true | all-gather | bytes 655360 | tf_op jit(solution)/shard_map/all_gather | solution.py:649
  267.7 2.0 chain_b2.1
  269.7 1.9 collective-permute-start.11
  271.6 1.3 collective-permute-start.12
  272.9 2.5 collective-permute-start.13
  275.4 7.8 %collective-permute-done.12 = f32[1,64,128]{2,1,0:T(8,128)S(1)} collective-permute-done((f32[1,64,128]{2,1,0:T(8,128)S(1)}, f32[1,64,128]{2,1,0:T(8,128)S(1)}, u32[]{:S(2)}, u32[]{:S(2)}) %collective-permute-start.12) | collective-permute-done | bytes 32800 | tf_op jit(solution)/shard_map/ppermute | solution.py:645
  283.3 8.1 %all-gather.7 = f32[16,64,128]{2,1,0:T(8,128)S(1)} all-gather(f32[4,64,128]{2,1,0:T(8,128)S(1)} %pad_maximum_fusion.2), channel_id=9, replica_groups=mesh['tm'=16,'gx'=4,'gy'=4] {'gx'}, dimensions={0}, use_global_device_ids=true | all-gather | bytes 655360 | tf_op jit(solution)/shard_map/all_gather | solution.py:654
  291.4 4.1 %chain_b4.1 = (f32[16,64,128]{2,1,0:T(8,128)S(1)}, f32[2,64,128]{2,1,0:T(8,128)S(1)}, f32[1,64,128]{2,1,0:T(8,128)S(1)}, f32[1,64,128]{2,1,0:T(8,128)S(1)}) custom-call(s32[1]{0:T(128)} %bitcast.place, f32[4,4,64,128]{3,2,1,0:T(8,128)S(1)} %bitcast.23, f32[16,64,128]{2,1,0:T(8,128)S(1)} %get-tuple-element.59.c_in, f32[16,64,128]{2,1,0:T(8,128)S(1)} %copy-done.2, ...), custom_call_target="tpu_custom_call" | custom-call | flops 100000000 | bytes 1000000 | tf_op jit(solution)/shard_map/chain_b4/pallas_call | solution.py:618
  295.5 1.3 collective-permute-start.14
  296.8 1.3 collective-permute-start.15
  298.7 6.8 %collective-permute-done.15 = f32[1,64,128]{2,1,0:T(8,128)S(1)} collective-permute-done((f32[1,64,128]{2,1,0:T(8,128)S(1)}, f32[1,64,128]{2,1,0:T(8,128)S(1)}, u32[]{:S(2)}, u32[]{:S(2)}) %collective-permute-start.15) | collective-permute-done | bytes 32800 | tf_op jit(solution)/shard_map/ppermute | solution.py:645
  305.5 8.0 %all-gather.8 = f32[16,64,128]{2,1,0:T(8,128)S(1)} all-gather(f32[4,64,128]{2,1,0:T(8,128)S(1)} %pad_maximum_fusion.3), channel_id=10, replica_groups=mesh['tm'=16,'gx'=4,'gy'=4] {'gx'}, dimensions={0}, use_global_device_ids=true | all-gather | bytes 655360 | tf_op jit(solution)/shard_map/all_gather | solution.py:654
  313.5 7.7 %finish.1 = f32[8,64,128]{2,1,0:T(8,128)S(1)} custom-call(s32[1]{0:T(128)} %bitcast.place, f32[4,4,64,128]{3,2,1,0:T(8,128)S(1)} %bitcast.24, f32[16,64,128]{2,1,0:T(8,128)S(1)} %get-tuple-element.63.c_in, f32[16,64,128]{2,1,0:T(8,128)S(1)} %copy-done.2, bf16[4,64,256]{2,1,0:T(8,128)(2,1)S(1)} %copy-done.5, f32[8,64,256]{2,1,0:T(8,128)S(1)} %copy-done.9), custom_call_target="tpu_custom_call" | custom-call | flops 100000000 | bytes 1000000 | tf_op jit(solution)/shard_map/finish/pallas_call | solution.py:618
  (54 shorter events, 7.6 us)
Async XLA Ops:
  6.5 36.1 %all-gather.12.cloned.1.call-start = ((), (), s32[]{:S(2)}) async-start(), calls=%async_computation | async-start | bytes 2785280 | tf_op jit(solution)/shard_map/all_gather | solution.py:689
  8.3 15.6 %copy-start.11 = (f32[8,1]{0,1:T(1,128)S(1)}, f32[8,1]{0,1:T(1,128)}, u32[]{:S(2)}) copy-start(f32[8,1]{0,1:T(1,128)} %param.11) | copy-start | bytes 100
  8.4 24.7 %copy-start.10 = (f32[64]{0:T(128)S(1)}, f32[64]{0:T(128)}, u32[]{:S(2)}) copy-start(f32[64]{0:T(128)} %param.8) | copy-start | bytes 772
  11.5 62.3 %all-gather.14.cloned.1.call-start = ((), (), s32[]{:S(2)}) async-start(), calls=%async_computation.1 | async-start | bytes 2785280 | tf_op jit(solution)/shard_map/all_gather | solution.py:690
  11.6 10.3 %collective-permute-start = (f32[4,136,128]{2,1,0:T(8,128)S(1)}, f32[4,136,128]{2,1,0:T(8,128)S(1)}, u32[]{:S(2)}, u32[]{:S(2)}) collective-permute-start(f32[4,136,128]{2,1,0:T(8,128)S(1)} %get-tuple-element.36), channel_id=1, source_target_pairs={{0,1},{1,2},{2,3},{16,17},{17,18},{18,19},{32,33},{33,34},{34,35},... | collective-permute-start | bytes 835592 | tf_op jit(solution)/shard_map/ppermute | solution.py:645
  12.9 10.2 %collective-permute-start.1 = (f32[4,136,128]{2,1,0:T(8,128)S(1)}, f32[4,136,128]{2,1,0:T(8,128)S(1)}, u32[]{:S(2)}, u32[]{:S(2)}) collective-permute-start(f32[4,136,128]{2,1,0:T(8,128)S(1)} %get-tuple-element.37), channel_id=1, source_target_pairs={{1,0},{2,1},{3,2},{17,16},{18,17},{19,18},{33,32},{34,33},{35,34},... | collective-permute-start | bytes 835592 | tf_op jit(solution)/shard_map/ppermute | solution.py:645
  24.0 11.0 %collective-permute-start.3 = (f32[8,1]{0,1:T(1,128)S(1)}, f32[8,1]{0,1:T(1,128)S(1)}, u32[]{:S(2)}, u32[]{:S(2)}) collective-permute-start(f32[8,1]{0,1:T(1,128)S(1)} %copy-done.11), channel_id=1, source_target_pairs={{0,32},{1,33},{2,34},{3,35},{16,48},{17,49},{18,50},{19,51},{32,64... | collective-permute-start | bytes 104 | tf_op jit(solution)/shard_map/ppermute | solution.py:645
  29.2 7.5 %collective-permute-start.2 = (f32[8,1]{0,1:T(1,128)S(1)}, f32[8,1]{0,1:T(1,128)S(1)}, u32[]{:S(2)}, u32[]{:S(2)}) collective-permute-start(f32[8,1]{0,1:T(1,128)S(1)} %copy-done.11), channel_id=1, source_target_pairs={{0,16},{1,17},{2,18},{3,19},{16,32},{17,33},{18,34},{19,35},{32,48... | collective-permute-start | bytes 104 | tf_op jit(solution)/shard_map/ppermute | solution.py:645
  33.7 0.7 copy-start.3
  74.6 75.7 %copy-start.4 = (bf16[4,64,256]{2,1,0:T(8,128)(2,1)S(1)}, bf16[4,64,256]{2,1,0:T(8,128)(2,1)}, u32[]{:S(2)}) copy-start(bf16[4,64,256]{2,1,0:T(8,128)(2,1)} %copy-done.3) | copy-start | bytes 393220
  128.9 48.6 %copy-start.1 = (f32[16,64,128]{2,1,0:T(8,128)S(1)}, f32[16,64,128]{2,1,0:T(8,128)}, u32[]{:S(2)}) copy-start(f32[16,64,128]{2,1,0:T(8,128)} %get-tuple-element.40.cc) | copy-start | bytes 1572868
  128.9 12.8 %collective-permute-start.4 = (f32[4,64,128]{2,1,0:T(8,128)}, f32[4,64,128]{2,1,0:T(8,128)S(1)}, u32[]{:S(2)}, u32[]{:S(2)}) collective-permute-start(f32[4,64,128]{2,1,0:T(8,128)} %get-tuple-element.38), channel_id=1, source_target_pairs={{0,32},{1,33},{2,34},{3,35},{16,48},{17,49},{18,50},{19,51},{32,64... | collective-permute-start | bytes 393224 | tf_op jit(solution)/shard_map/ppermute | solution.py:645
  150.3 1.0 copy-start
  151.3 1.0 copy-start.7
  154.3 14.7 %collective-permute-start.5 = (f32[4,64,128]{2,1,0:T(8,128)S(1)}, f32[4,64,128]{2,1,0:T(8,128)S(1)}, u32[]{:S(2)}, u32[]{:S(2)}) collective-permute-start(f32[4,64,128]{2,1,0:T(8,128)S(1)} %get-tuple-element.41), channel_id=1, source_target_pairs={{0,64},{1,65},{2,66},{3,67},{16,80},{17,81},{18,82},{19,83},{32,96... | collective-permute-start | bytes 393224 | tf_op jit(solution)/shard_map/ppermute | solution.py:645
  181.2 16.5 %copy-start.6 = (f32[16,64,128]{2,1,0:T(8,128)}, f32[16,64,128]{2,1,0:T(8,128)S(1)}, u32[]{:S(2)}) copy-start(f32[16,64,128]{2,1,0:T(8,128)S(1)} %get-tuple-element.46.c_in) | copy-start | bytes 1572868
  181.2 8.0 %collective-permute-start.6 = (f32[2,64,128]{2,1,0:T(8,128)S(1)}, f32[2,64,128]{2,1,0:T(8,128)S(1)}, u32[]{:S(2)}, u32[]{:S(2)}) collective-permute-start(f32[2,64,128]{2,1,0:T(8,128)S(1)} %get-tuple-element.43), channel_id=1, source_target_pairs={{0,128},{1,129},{2,130},{3,131},{16,144},{17,145},{18,146},{19,147... | collective-permute-start | bytes 196616 | tf_op jit(solution)/shard_map/ppermute | solution.py:645
  182.5 6.7 %collective-permute-start.7 = (f32[1,64,128]{2,1,0:T(8,128)S(1)}, f32[1,64,128]{2,1,0:T(8,128)S(1)}, u32[]{:S(2)}, u32[]{:S(2)}) collective-permute-start(f32[1,64,128]{2,1,0:T(8,128)S(1)} %get-tuple-element.44), channel_id=1, source_target_pairs={{0,129},{1,130},{2,131},{16,145},{17,146},{18,147},{32,161},{33,16... | collective-permute-start | bytes 98312 | tf_op jit(solution)/shard_map/ppermute | solution.py:645
  183.8 5.4 %collective-permute-start.8 = (f32[1,64,128]{2,1,0:T(8,128)S(1)}, f32[1,64,128]{2,1,0:T(8,128)S(1)}, u32[]{:S(2)}, u32[]{:S(2)}) collective-permute-start(f32[1,64,128]{2,1,0:T(8,128)S(1)} %get-tuple-element.45), channel_id=1, source_target_pairs={{1,128},{2,129},{3,130},{17,144},{18,145},{19,146},{33,160},{34,16... | collective-permute-start | bytes 98312 | tf_op jit(solution)/shard_map/ppermute | solution.py:645
  197.7 47.0 %copy-start.2 = (f32[16,64,128]{2,1,0:T(8,128)S(1)}, f32[16,64,128]{2,1,0:T(8,128)}, u32[]{:S(2)}) copy-start(f32[16,64,128]{2,1,0:T(8,128)} %get-tuple-element.40.cc) | copy-start | bytes 1572868
  197.7 47.0 %copy-start.5 = (bf16[4,64,256]{2,1,0:T(8,128)(2,1)S(1)}, bf16[4,64,256]{2,1,0:T(8,128)(2,1)}, u32[]{:S(2)}) copy-start(bf16[4,64,256]{2,1,0:T(8,128)(2,1)} %copy-done.3) | copy-start | bytes 393220
  226.8 10.0 %collective-permute-start.9 = (f32[4,64,128]{2,1,0:T(8,128)}, f32[4,64,128]{2,1,0:T(8,128)S(1)}, u32[]{:S(2)}, u32[]{:S(2)}) collective-permute-start(f32[4,64,128]{2,1,0:T(8,128)} %get-tuple-element.52), channel_id=1, source_target_pairs={{0,16},{1,17},{2,18},{3,19},{16,32},{17,33},{18,34},{19,35},{32,48... | collective-permute-start | bytes 393224 | tf_op jit(solution)/shard_map/ppermute | solution.py:645
  244.7 1.0 copy-start.8
  246.7 12.6 %collective-permute-start.10 = (f32[4,64,128]{2,1,0:T(8,128)S(1)}, f32[4,64,128]{2,1,0:T(8,128)S(1)}, u32[]{:S(2)}, u32[]{:S(2)}) collective-permute-start(f32[4,64,128]{2,1,0:T(8,128)S(1)} %get-tuple-element.54), channel_id=1, source_target_pairs={{0,32},{1,33},{2,34},{3,35},{16,48},{17,49},{18,50},{19,51},{32,64... | collective-permute-start | bytes 393224 | tf_op jit(solution)/shard_map/ppermute | solution.py:645
  267.7 45.8 %copy-start.9 = (f32[8,64,256]{2,1,0:T(8,128)S(1)}, f32[8,64,256]{2,1,0:T(8,128)}, u32[]{:S(2)}) copy-start(f32[8,64,256]{2,1,0:T(8,128)} %get-tuple-element.64.v_tile) | copy-start | bytes 1572868
  269.7 13.6 %collective-permute-start.11 = (f32[2,64,128]{2,1,0:T(8,128)S(1)}, f32[2,64,128]{2,1,0:T(8,128)S(1)}, u32[]{:S(2)}, u32[]{:S(2)}) collective-permute-start(f32[2,64,128]{2,1,0:T(8,128)S(1)} %get-tuple-element.56), channel_id=1, source_target_pairs={{0,64},{1,65},{2,66},{3,67},{16,80},{17,81},{18,82},{19,83},{32,96... | collective-permute-start | bytes 196616 | tf_op jit(solution)/shard_map/ppermute | solution.py:645
  271.6 11.6 %collective-permute-start.12 = (f32[1,64,128]{2,1,0:T(8,128)S(1)}, f32[1,64,128]{2,1,0:T(8,128)S(1)}, u32[]{:S(2)}, u32[]{:S(2)}) collective-permute-start(f32[1,64,128]{2,1,0:T(8,128)S(1)} %get-tuple-element.57), channel_id=1, source_target_pairs={{0,65},{1,66},{2,67},{16,81},{17,82},{18,83},{32,97},{33,98},{34,9... | collective-permute-start | bytes 98312 | tf_op jit(solution)/shard_map/ppermute | solution.py:645
  272.9 10.3 %collective-permute-start.13 = (f32[1,64,128]{2,1,0:T(8,128)S(1)}, f32[1,64,128]{2,1,0:T(8,128)S(1)}, u32[]{:S(2)}, u32[]{:S(2)}) collective-permute-start(f32[1,64,128]{2,1,0:T(8,128)S(1)} %get-tuple-element.58), channel_id=1, source_target_pairs={{1,64},{2,65},{3,66},{17,80},{18,81},{19,82},{33,96},{34,97},{35,9... | collective-permute-start | bytes 98312 | tf_op jit(solution)/shard_map/ppermute | solution.py:645
  295.5 10.0 %collective-permute-start.14 = (f32[2,64,128]{2,1,0:T(8,128)S(1)}, f32[2,64,128]{2,1,0:T(8,128)S(1)}, u32[]{:S(2)}, u32[]{:S(2)}) collective-permute-start(f32[2,64,128]{2,1,0:T(8,128)S(1)} %get-tuple-element.60), channel_id=1, source_target_pairs={{0,128},{1,129},{2,130},{3,131},{16,144},{17,145},{18,146},{19,147... | collective-permute-start | bytes 196616 | tf_op jit(solution)/shard_map/ppermute | solution.py:645
  296.8 8.7 %collective-permute-start.15 = (f32[1,64,128]{2,1,0:T(8,128)S(1)}, f32[1,64,128]{2,1,0:T(8,128)S(1)}, u32[]{:S(2)}, u32[]{:S(2)}) collective-permute-start(f32[1,64,128]{2,1,0:T(8,128)S(1)} %get-tuple-element.61), channel_id=1, source_target_pairs={{0,129},{1,130},{2,131},{16,145},{17,146},{18,147},{32,161},{33,16... | collective-permute-start | bytes 98312 | tf_op jit(solution)/shard_map/ppermute | solution.py:645
  298.1 7.4 %collective-permute-start.16 = (f32[1,64,128]{2,1,0:T(8,128)S(1)}, f32[1,64,128]{2,1,0:T(8,128)S(1)}, u32[]{:S(2)}, u32[]{:S(2)}) collective-permute-start(f32[1,64,128]{2,1,0:T(8,128)S(1)} %get-tuple-element.62), channel_id=1, source_target_pairs={{1,128},{2,129},{3,130},{17,144},{18,145},{19,146},{33,160},{34,16... | collective-permute-start | bytes 98312 | tf_op jit(solution)/shard_map/ppermute | solution.py:645
Sparse Core Ops, SparseCore 0:
  11.7 30.9 all-gather.11
  44.5 29.3 all-gather.13
